TPU v7x, 32 devices: a whole 2x2x4 slice. The times are simulated.
32 devices in a mesh: seq: 16 (over z, y, x), head: 2 (over core).
Axes of the slice: x: 2, y: 2, z: 4, core: 2. Of those that a mesh axis runs over, the one named last changes fastest.
Arguments:
- query_rows: bfloat16 [6144, 2048], P('seq', 'head'), may hold values from -41 to 41
- key_rows: bfloat16 [6144, 2048], P('seq', 'head'), may hold values from -4 to 4, as said below
- value_rows: bfloat16 [6144, 2048], P('seq', 'head'), may hold values from -6 to 6
- out_grad: bfloat16 [6144, 2048], P('seq'), may hold values from -6 to 6
- cluster_ids: int32 [16, 6144, 1], P('head', 'seq'), may hold values from 0 to 255; in each aligned block of 384 rows (0 to 383, 384 to 767, ..., all dimensions but the last counted through in order) at most 2 rows name the same one
- out_weight: bfloat16 [2048, 2048], P('head'), may hold values from -0.125 to 0.125
Outputs:
- layer_out: bfloat16 [6144, 2048], P('seq', 'head')
- query_grad: bfloat16 [6144, 2048], P('seq', 'head')
- key_grad: bfloat16 [6144, 2048], P('seq', 'head')
- value_grad: bfloat16 [6144, 2048], P('seq', 'head')
Inputs may be any that keep to these rules, and one draw needn't show every extreme that they name: `cluster_ids`: in each head the 384 tokens of one index of seq (aligned blocks of the token dimension) name no cluster more than 2 times, a bound that some block reaches in every draw. `key_rows`: no token's key in any head is all zeros.
All inputs are finite; a program needn't handle non-finite values.
Results may differ from a plain program's by a relative error of at most 0.009.
Values may be sent and summed in bfloat16 or wider, within the bound.
A program may use at most 128 MiB of HBM per device.

v0:
```python
import functools

import jax
import jax.numpy as jnp
from jax import lax
from jax.experimental import pallas as pl
from jax.experimental.pallas import tpu as pltpu
from jax.sharding import PartitionSpec as P

CLUSTERS = 256
MOST = 2
QUARTERS = 4
LAG = 4
NEGATIVE = -1e30
MESH = pl.DeviceIdType.MESH
F32 = jnp.float32
BF16 = jnp.bfloat16


def dot(a, b, da, db):
    return lax.dot_general(a, b, (((da,), (db,)), ((), ())), preferred_element_type=F32)


def kernel(
    spots, heads, dh, nh,
    query, key, value, grad, ids_row, ids_col, weight,
    layer_out, query_grad, key_grad, value_grad,
    onehot, send, got, kv, zin, zup, zdown, back, total, half_out, half_in,
    as_, ar, kvs, kvr, zs, zr, bs, br, hs, hr,
):
    tokens = query.shape[0]
    slots = CLUSTERS * MOST
    rows = slots // spots
    step = 16
    tiles = rows // step
    quarter = spots * step
    two = 2 * dh
    four = 4 * dh
    scale = dh ** -0.5
    seq = lax.axis_index("seq")
    hd = lax.axis_index("head")
    z = seq // spots
    r = seq % spots

    def peer(k):
        return z * spots + (r + k) % spots

    barrier = pltpu.get_barrier_semaphore()
    for k in range(1, spots):
        pl.semaphore_signal(barrier, inc=1, device_id={"seq": peer(k)}, device_id_type=MESH)
    for k in range(1, nh):
        pl.semaphore_signal(barrier, inc=1, device_id={"head": (hd + k) % nh}, device_id_type=MESH)

    whole = QUARTERS * spots
    for to in ((seq + spots) % whole, (seq + whole - spots) % whole):
        pl.semaphore_signal(barrier, inc=1, device_id={"seq": to}, device_id_type=MESH)
    pl.semaphore_wait(barrier, spots - 1 + nh - 1 + 2)

    def remote(src, dst, ss, rs, to):
        return pltpu.make_async_remote_copy(
            src_ref=src, dst_ref=dst, send_sem=ss, recv_sem=rs,
            device_id={"seq": to}, device_id_type=MESH,
        )

    def out_copy(h, k):
        d = (r + k) % spots
        return remote(send.at[h, d], got.at[h, r], as_.at[h, k], ar.at[h, k], peer(k))

    def in_copy(h, k):
        s = (r + spots - k) % spots
        return remote(send.at[h, s], got.at[h, s], as_.at[h, k], ar.at[h, k], peer(k))

    def back_copy(h, k):
        d = (r + k) % spots
        return remote(send.at[h, d], back.at[h, r], bs.at[h, k], br.at[h, k], peer(k))

    def back_in(h, k):
        s = (r + spots - k) % spots
        return remote(send.at[h, s], back.at[h, s], bs.at[h, k], br.at[h, k], peer(k))

    low = pl.ds(0, two)
    high = pl.ds(two, two)
    above = jnp.minimum(seq + spots, QUARTERS * spots - 1)
    below = jnp.maximum(seq - spots, 0)

    def kv_first(h):
        return remote(got.at[h, :, :, low], kv.at[h, :, :, low], kvs.at[h, 1], kvr.at[h, 0], above)

    def kv_own(h):
        return remote(got.at[h, :, :, low], kv.at[h, :, :, high], kvs.at[h, 1], kvr.at[h, 1], above)

    def kv_forward(h):
        return remote(kv.at[h, :, :, low], kv.at[h, :, :, low], kvs.at[h, 0], kvr.at[h, 0], above)

    def top_down(h):
        return remote(got.at[h], zin.at[h], zs.at[h, 0], zr.at[h], below)

    def top_back(h):
        return remote(zup.at[h], zin.at[h], zs.at[h, 0], zr.at[h], above)

    def sums_down(h):
        return remote(zdown.at[h], zin.at[h], zs.at[h, 1], zr.at[h], below)

    def last_down(h):
        return remote(zdown.at[h, :, :, low], zin.at[h, :, :, low], zs.at[h, 1], zr.at[h], below)

    def columns(h):
        return pl.ds(pl.multiple_of(h * dh, dh), dh)

    def fill(h, carry):
        cols = columns(h)
        row = ids_row[h]
        col = ids_col[h]
        at0 = lax.broadcasted_iota(jnp.int32, (tokens, tokens), 0)
        at1 = lax.broadcasted_iota(jnp.int32, (tokens, tokens), 1)
        same = jnp.logical_and(col == row, at0 < at1)
        before = jnp.sum(jnp.where(same, 1, 0), axis=0, keepdims=True)
        slot = row * MOST + before
        place = lax.broadcasted_iota(jnp.int32, (slots, tokens), 0)
        picked = jnp.where(place == slot, 1.0, 0.0).astype(BF16)
        onehot[h] = picked
        attn_grad = dot(grad[...], weight[cols, :], 1, 1).astype(BF16)
        for c, x in enumerate((key[:, cols], value[:, cols], query[:, cols], attn_grad)):
            send[h, :, :, c * dh:(c + 1) * dh] = dot(picked, x, 1, 0).astype(BF16).reshape(spots, rows, dh)
        for k in range(1, spots):
            out_copy(h, k).start()
        got[h, r] = send[h, r]
        return carry

    lax.fori_loop(0, heads, fill, 0)
    total[...] = jnp.zeros_like(total)

    chunk = min(spots, 4)
    chunks = spots // chunk

    def attend(h, g, nk, both):
        at = pl.ds(pl.multiple_of(g * step, step), step)
        flat = lambda x: x.reshape(x.shape[0] * step, x.shape[2])
        own = flat(got[h, :, at, low])
        if both:
            parts = [flat(kv[h, :, at, low]), flat(kv[h, :, at, high]), own, flat(zin[h, :, at, low])]
        elif nk == 2:
            parts = [flat(kv[h, :, at, low]), own]
        else:
            parts = [own]
        kvs_all = jnp.concatenate(parts, axis=0) if nk > 1 else own
        keys, values = kvs_all[:, :dh], kvs_all[:, dh:]
        nkeys = nk * quarter
        nq = chunk * step * (2 if both else 1)
        j = lax.broadcasted_iota(jnp.int32, (nkeys, 1), 0)
        occupied = jnp.max(jnp.abs(keys.astype(F32)), axis=1, keepdims=True) > 0
        cluster_k = jnp.where(occupied, (j & 15) >> 1, -1)
        rank_k = (j >> 4) * 2 + (j & 1)
        i = lax.broadcasted_iota(jnp.int32, (1, nq), 1)
        cluster_q = (i & 15) >> 1
        own_at = nk - (2 if both else 1)

        def part(c):
            if chunks == 1:
                mine = slice(None)
            else:
                mine = pl.ds(c * chunk, chunk)
            qg = flat(got[h, mine, at, high])
            if both:
                qg = jnp.concatenate([qg, flat(zin[h, mine, at, high])], axis=0)
            q, dout = qg[:, :dh], qg[:, dh:]
            if both:
                second = (i >= chunk * step).astype(jnp.int32)
            else:
                second = 0
            src = c * chunk + ((i - second * (chunk * step)) >> 4)
            rank_q = ((own_at + second) * spots + src) * 2 + (i & 1)
            allowed = jnp.logical_and(cluster_k == cluster_q, rank_k <= rank_q)
            scores = jnp.where(allowed, dot(keys, q, 1, 1) * scale, NEGATIVE)
            w = jnp.exp(scores - jnp.max(scores, axis=0, keepdims=True))
            probs = w * (1.0 / jnp.sum(w, axis=0, keepdims=True))
            probs_half = probs.astype(BF16)
            dprob = dot(values, dout, 1, 1)
            delta = jnp.sum(probs * dprob, axis=0, keepdims=True)
            dscore = (probs * (dprob - delta)).astype(BF16)
            dq = (dot(dscore, keys, 0, 0) * scale).astype(BF16)
            attn = dot(probs_half, values, 0, 0).astype(BF16)
            half = chunk * step
            for x, c0 in ((dq, two), (attn, two + dh)):
                send[h, mine, at, c0:c0 + dh] = x[:half].reshape(chunk, step, dh)
                if both:
                    zup[h, mine, at, c0:c0 + dh] = x[half:].reshape(chunk, step, dh)
            return dot(dscore, q, 1, 0) * scale, dot(probs_half, dout, 1, 0)

        if chunks == 1:
            dk, dv = part(0)
        else:
            def more(c, sums):
                a, b = part(c)
                return sums[0] + a, sums[1] + b
            zero = jnp.zeros((nkeys, dh), F32)
            dk, dv = lax.fori_loop(0, chunks, more, (zero, zero))
        for x, c0 in ((dk.astype(BF16), 0), (dv.astype(BF16), dh)):
            cut = lambda a: x[a * quarter:(a + 1) * quarter].reshape(spots, step, dh)
            send[h, :, at, c0:c0 + dh] = cut(own_at)
            if nk > 1:
                zdown[h, :, at, c0:c0 + dh] = cut(0)
            if both:
                zdown[h, :, at, two + c0:two + c0 + dh] = cut(1)
                zup[h, :, at, c0:c0 + dh] = cut(3)

    def attend_all(h, nk, both):
        def one(g, carry):
            attend(h, g, nk, both)
            return carry
        lax.fori_loop(0, tiles, one, 0)

    def push(h):
        for k in range(1, spots):
            in_copy(h, k).wait_recv()
        for k in range(1, spots):
            out_copy(h, k).wait_send()

        @pl.when(z == 0)
        def _():
            kv_first(h).start()
            attend_all(h, 1, False)

        @pl.when(z == 1)
        def _():
            kv_own(h).start()
            kv_forward(h).wait_recv()
            kv_forward(h).start()
            attend_all(h, 2, False)

        @pl.when(z == 2)
        def _():
            kv_forward(h).wait_recv()
            kv_own(h).wait_recv()
            top_down(h).wait_recv()
            attend_all(h, 4, True)
            sums_down(h).start()
            top_back(h).start()

        @pl.when(z == 3)
        def _():
            top_down(h).start()

    def give_back(h):
        @pl.when(z == 0)
        def _():
            last_down(h).wait_recv()
            send[h, :, :, low] = (send[h, :, :, low].astype(F32) + zin[h, :, :, low].astype(F32)).astype(BF16)

        @pl.when(z == 1)
        def _():
            sums_down(h).wait_recv()
            zdown[h, :, :, low] = (zdown[h, :, :, low].astype(F32) + zin[h, :, :, low].astype(F32)).astype(BF16)
            last_down(h).start()
            send[h, :, :, low] = (send[h, :, :, low].astype(F32) + zin[h, :, :, high].astype(F32)).astype(BF16)

        @pl.when(z == 3)
        def _():
            top_back(h).wait_recv()
            send[h] = zin[h]

        for k in range(1, spots):
            back_copy(h, k).start()
        back[h, r] = send[h, r]

    def finish(h):
        cols = columns(h)
        for k in range(1, spots):
            back_in(h, k).wait_recv()
        picked = onehot[h]
        for c, out in ((0, key_grad), (1, value_grad), (2, query_grad)):
            block = back[h, :, :, c * dh:(c + 1) * dh].reshape(slots, dh)
            out[:, cols] = dot(picked, block, 0, 0).astype(BF16)
        attn = dot(picked, back[h, :, :, 3 * dh:four].reshape(slots, dh), 0, 0).astype(BF16)
        total[...] += dot(attn, weight[cols, :], 1, 0)

    def turn(i, carry):
        @pl.when(i < heads)
        def _():
            push(i)

        @pl.when(i >= LAG + 1)
        def _():
            finish(i - LAG - 1)

        @pl.when(jnp.logical_and(i >= LAG, i < heads + LAG))
        def _():
            give_back(i - LAG)

        return carry

    lax.fori_loop(0, heads + LAG + 1, turn, 0)

    width = layer_out.shape[1]

    def share(k):
        return pltpu.make_async_remote_copy(
            src_ref=half_out.at[k - 1], dst_ref=half_in.at[k - 1],
            send_sem=hs.at[k - 1], recv_sem=hr.at[k - 1],
            device_id={"head": (hd + k) % nh}, device_id_type=MESH,
        )

    for k in range(1, nh):
        to = (hd + k) % nh
        half_out[k - 1] = total[:, pl.ds(pl.multiple_of(to * width, width), width)].astype(BF16)
        share(k).start()
    mine = total[:, pl.ds(pl.multiple_of(hd * width, width), width)]

    def settle(h, carry):
        for k in range(1, spots):
            back_copy(h, k).wait_send()

        @pl.when(z == 0)
        def _():
            kv_first(h).wait_send()

        @pl.when(z == 1)
        def _():
            kv_own(h).wait_send()
            kv_forward(h).wait_send()
            last_down(h).wait_send()

        @pl.when(z == 2)
        def _():
            sums_down(h).wait_send()
            top_back(h).wait_send()

        @pl.when(z == 3)
        def _():
            top_down(h).wait_send()

        return carry

    lax.fori_loop(0, heads, settle, 0)
    for k in range(1, nh):
        share(k).wait()
        mine = mine + half_in[k - 1].astype(F32)
    layer_out[...] = mine.astype(BF16)


def body(nseq, nh, query_rows, key_rows, value_rows, out_grad, cluster_ids, out_weight):
    tokens, wide = query_rows.shape
    heads = cluster_ids.shape[0]
    dh = wide // heads
    spots = nseq // QUARTERS
    rows = CLUSTERS * MOST // spots
    model = out_weight.shape[1]
    out = jax.ShapeDtypeStruct((tokens, wide), BF16)
    vm = pl.BlockSpec(memory_space=pltpu.VMEM)
    full = pltpu.VMEM((heads, spots, rows, 4 * dh), BF16)
    dma = pltpu.SemaphoreType.DMA
    width = model // nh
    return pl.pallas_call(
        functools.partial(kernel, spots, heads, dh, nh),
        out_shape=(jax.ShapeDtypeStruct((tokens, width), BF16), out, out, out),
        in_specs=[vm] * 7,
        out_specs=(vm,) * 4,
        scratch_shapes=[
            pltpu.VMEM((heads, CLUSTERS * MOST, tokens), BF16),
            full, full, full, full, full, full, full,
            pltpu.VMEM((tokens, model), F32),
            pltpu.VMEM((nh - 1, tokens, width), BF16),
            pltpu.VMEM((nh - 1, tokens, width), BF16),
            dma((heads, spots)), dma((heads, spots)),
            dma((heads, 2)), dma((heads, 2)),
            dma((heads, 2)), dma((heads,)),
            dma((heads, spots)), dma((heads, spots)),
            dma((nh - 1,)), dma((nh - 1,)),
        ],
        compiler_params=pltpu.CompilerParams(
            collective_id=0, has_side_effects=True, vmem_limit_bytes=60 * 2**20
        ),
        cost_estimate=pl.CostEstimate(flops=10**10, bytes_accessed=2**24, transcendentals=2**21),
    )(
        query_rows, key_rows, value_rows, out_grad,
        cluster_ids.reshape(heads, 1, tokens), cluster_ids, out_weight,
    )


def solution(mesh):
    in_specs = (
        P("seq", "head"),
        P("seq", "head"),
        P("seq", "head"),
        P("seq", None),
        P("head", "seq", None),
        P("head", None),
    )
    out_specs = (P("seq", "head"), P("seq", "head"), P("seq", "head"), P("seq", "head"))
    run = functools.partial(body, mesh.shape["seq"], mesh.shape["head"])
    return jax.shard_map(run, mesh=mesh, in_specs=in_specs, out_specs=out_specs, check_vma=False)
```

profile of v0, /device:TPU:17, one launch (start us, length us, event | category | flops | bytes accessed | tf_op | source)
XLA Modules:
  0.0 169.3 jit_solution(3292416910797795813)
XLA Ops:
  0.6 2.4 %copy.10.ids_col = s32[8,384,1]{2,1,0:T(8,128)} copy(s32[8,384,1]{1,2,0:T(1,128)} %param.10) | data formatting | bytes 24576 | tf_op args[4]
  3.0 161.4 %shard_map.93 = (bf16[384,1024]{1,0:T(8,128)(2,1)}, bf16[384,1024]{1,0:T(8,128)(2,1)}, bf16[384,1024]{1,0:T(8,128)(2,1)}, bf16[384,1024]{1,0:T(8,128)(2,1)}) custom-call(bf16[384,1024]{1,0:T(8,128)(2,1)} %query.1, bf16[384,1024]{1,0:T(8,128)(2,1)} %key.1, bf16[384,1024]{1,0:T(8,128)(2,1)} %value.1, bf16[384,2048]{1,0:T(8,128)(2,1)} %grad.1, ...), custom_call_target="tpu_custom_call" | custom-call | flops 10000000000 | bytes 16777216 | tf_op jit(solution)/shard_map/pallas_call | solution.py:353
  164.4 0.0 copy-start.2
  164.4 0.0 copy-start.1
  164.4 2.2 %copy.15 = bf16[384,1024]{1,0:T(8,128)(2,1)} copy(bf16[384,1024]{1,0:T(8,128)(2,1)} %get-tuple-element.8) | data formatting | bytes 1572864
  166.6 0.0 copy-done.2
  166.6 0.0 copy-start
  166.6 0.9 copy.16
  167.5 0.0 copy-done.1
  167.5 0.9 copy.17
  168.4 0.0 copy-done
  168.4 0.9 copy.18
Async XLA Ops:
  164.4 2.2 %copy-start.2 = (bf16[384,1024]{1,0:T(8,128)(2,1)S(1)}, bf16[384,1024]{1,0:T(8,128)(2,1)}, u32[]{:S(2)}) copy-start(bf16[384,1024]{1,0:T(8,128)(2,1)} %get-tuple-element.9) | copy-start | bytes 2359300
  164.4 3.1 %copy-start.1 = (bf16[384,1024]{1,0:T(8,128)(2,1)S(1)}, bf16[384,1024]{1,0:T(8,128)(2,1)}, u32[]{:S(2)}) copy-start(bf16[384,1024]{1,0:T(8,128)(2,1)} %get-tuple-element.10) | copy-start | bytes 2359300
  166.6 1.8 %copy-start = (bf16[384,1024]{1,0:T(8,128)(2,1)S(1)}, bf16[384,1024]{1,0:T(8,128)(2,1)}, u32[]{:S(2)}) copy-start(bf16[384,1024]{1,0:T(8,128)(2,1)} %get-tuple-element.11) | copy-start | bytes 2359300
where the time goes:
time: 170 us; the launch traced here: 169 us
  Pallas kernels  161 us (95%)
  local copies, waits for them, and re-layouts  7.21 us (4%)
    pallas_call x1, Pallas kernels, body(): pl.pallas_call(functools.partial(kernel, spots, heads, dh, nh), out_shape...  161 us
    unnamed x11, local copies, waits for them, and re-layouts  7.21 us

commit v1 on v0

--- a/solution.py
+++ b/solution.py
@@ -10,7 +10,7 @@
 CLUSTERS = 256
 MOST = 2
 QUARTERS = 4
-LAG = 4
+LAG = 6
 NEGATIVE = -1e30
 MESH = pl.DeviceIdType.MESH
 F32 = jnp.float32
@@ -22,15 +22,16 @@
 
 
 def kernel(
-    spots, heads, dh, nh,
-    query, key, value, grad, ids_row, ids_col, weight,
+    spots, heads, split, dh, nh,
+    query, key, value, grad, ids_row, weight,
     layer_out, query_grad, key_grad, value_grad,
-    onehot, send, got, kv, zin, zup, zdown, back, total, half_out, half_in,
+    onehot, earlier, attn_all, send, got, kv, zin, zup, zdown, back, total, half_out, half_in,
     as_, ar, kvs, kvr, zs, zr, bs, br, hs, hr,
 ):
     tokens = query.shape[0]
     slots = CLUSTERS * MOST
-    rows = slots // spots
+    rows = slots // spots // split
+    units = heads * split
     step = 16
     tiles = rows // step
     quarter = spots * step
@@ -107,24 +108,29 @@
     def columns(h):
         return pl.ds(pl.multiple_of(h * dh, dh), dh)
 
+    at0 = lax.broadcasted_iota(jnp.int32, (tokens, tokens), 0)
+    at1 = lax.broadcasted_iota(jnp.int32, (tokens, tokens), 1)
+    earlier[...] = jnp.where(at0 < at1, 1.0, 0.0).astype(BF16)
+
     def fill(h, carry):
         cols = columns(h)
         row = ids_row[h]
-        col = ids_col[h]
-        at0 = lax.broadcasted_iota(jnp.int32, (tokens, tokens), 0)
-        at1 = lax.broadcasted_iota(jnp.int32, (tokens, tokens), 1)
-        same = jnp.logical_and(col == row, at0 < at1)
-        before = jnp.sum(jnp.where(same, 1, 0), axis=0, keepdims=True)
+        named = lax.broadcasted_iota(jnp.int32, (CLUSTERS, tokens), 0) == row
+        counts = dot(jnp.where(named, 1.0, 0.0).astype(BF16), earlier[...], 1, 0)
+        before = jnp.sum(jnp.where(named, counts, 0.0), axis=0, keepdims=True).astype(jnp.int32)
         slot = row * MOST + before
         place = lax.broadcasted_iota(jnp.int32, (slots, tokens), 0)
         picked = jnp.where(place == slot, 1.0, 0.0).astype(BF16)
         onehot[h] = picked
         attn_grad = dot(grad[...], weight[cols, :], 1, 1).astype(BF16)
-        for c, x in enumerate((key[:, cols], value[:, cols], query[:, cols], attn_grad)):
-            send[h, :, :, c * dh:(c + 1) * dh] = dot(picked, x, 1, 0).astype(BF16).reshape(spots, rows, dh)
-        for k in range(1, spots):
-            out_copy(h, k).start()
-        got[h, r] = send[h, r]
+        wide = jnp.concatenate([key[:, cols], value[:, cols], query[:, cols], attn_grad], axis=1)
+        table = dot(picked, wide, 1, 0).astype(BF16).reshape(spots, split, rows, four)
+        for part in range(split):
+            u = h * split + part
+            send[u] = table[:, part]
+            for k in range(1, spots):
+                out_copy(u, k).start()
+            got[u, r] = send[u, r]
         return carry
 
     lax.fori_loop(0, heads, fill, 0)
@@ -133,9 +139,11 @@
     chunk = min(spots, 4)
     chunks = spots // chunk
 
+    def flat(x):
+        return x.reshape(x.shape[0] * step, x.shape[2])
+
     def attend(h, g, nk, both):
         at = pl.ds(pl.multiple_of(g * step, step), step)
-        flat = lambda x: x.reshape(x.shape[0] * step, x.shape[2])
         own = flat(got[h, :, at, low])
         if both:
             parts = [flat(kv[h, :, at, low]), flat(kv[h, :, at, high]), own, flat(zin[h, :, at, low])]
@@ -146,7 +154,8 @@
         kvs_all = jnp.concatenate(parts, axis=0) if nk > 1 else own
         keys, values = kvs_all[:, :dh], kvs_all[:, dh:]
         nkeys = nk * quarter
-        nq = chunk * step * (2 if both else 1)
+        half = chunk * step
+        nq = half * (2 if both else 1)
         j = lax.broadcasted_iota(jnp.int32, (nkeys, 1), 0)
         occupied = jnp.max(jnp.abs(keys.astype(F32)), axis=1, keepdims=True) > 0
         cluster_k = jnp.where(occupied, (j & 15) >> 1, -1)
@@ -154,49 +163,42 @@
         i = lax.broadcasted_iota(jnp.int32, (1, nq), 1)
         cluster_q = (i & 15) >> 1
         own_at = nk - (2 if both else 1)
-
-        def part(c):
-            if chunks == 1:
-                mine = slice(None)
-            else:
-                mine = pl.ds(c * chunk, chunk)
+        dk = dv = None
+        for c in range(chunks):
+            mine = pl.ds(c * chunk, chunk)
             qg = flat(got[h, mine, at, high])
             if both:
                 qg = jnp.concatenate([qg, flat(zin[h, mine, at, high])], axis=0)
             q, dout = qg[:, :dh], qg[:, dh:]
-            if both:
-                second = (i >= chunk * step).astype(jnp.int32)
-            else:
-                second = 0
-            src = c * chunk + ((i - second * (chunk * step)) >> 4)
+            yield
+            raw = dot(keys, q, 1, 1)
+            dprob = dot(values, dout, 1, 1)
+            yield
+            second = (i >= half).astype(jnp.int32) if both else 0
+            src = c * chunk + ((i - second * half) >> 4)
             rank_q = ((own_at + second) * spots + src) * 2 + (i & 1)
             allowed = jnp.logical_and(cluster_k == cluster_q, rank_k <= rank_q)
-            scores = jnp.where(allowed, dot(keys, q, 1, 1) * scale, NEGATIVE)
+            scores = jnp.where(allowed, raw * scale, NEGATIVE)
             w = jnp.exp(scores - jnp.max(scores, axis=0, keepdims=True))
             probs = w * (1.0 / jnp.sum(w, axis=0, keepdims=True))
             probs_half = probs.astype(BF16)
-            dprob = dot(values, dout, 1, 1)
             delta = jnp.sum(probs * dprob, axis=0, keepdims=True)
             dscore = (probs * (dprob - delta)).astype(BF16)
+            yield
             dq = (dot(dscore, keys, 0, 0) * scale).astype(BF16)
             attn = dot(probs_half, values, 0, 0).astype(BF16)
-            half = chunk * step
+            more_k = dot(dscore, q, 1, 0)
+            more_v = dot(probs_half, dout, 1, 0)
+            dk = more_k if dk is None else dk + more_k
+            dv = more_v if dv is None else dv + more_v
+            yield
             for x, c0 in ((dq, two), (attn, two + dh)):
                 send[h, mine, at, c0:c0 + dh] = x[:half].reshape(chunk, step, dh)
                 if both:
                     zup[h, mine, at, c0:c0 + dh] = x[half:].reshape(chunk, step, dh)
-            return dot(dscore, q, 1, 0) * scale, dot(probs_half, dout, 1, 0)
-
-        if chunks == 1:
-            dk, dv = part(0)
-        else:
-            def more(c, sums):
-                a, b = part(c)
-                return sums[0] + a, sums[1] + b
-            zero = jnp.zeros((nkeys, dh), F32)
-            dk, dv = lax.fori_loop(0, chunks, more, (zero, zero))
-        for x, c0 in ((dk.astype(BF16), 0), (dv.astype(BF16), dh)):
-            cut = lambda a: x[a * quarter:(a + 1) * quarter].reshape(spots, step, dh)
+        for x, c0 in (((dk * scale).astype(BF16), 0), (dv.astype(BF16), dh)):
+            def cut(a):
+                return x[a * quarter:(a + 1) * quarter].reshape(spots, step, dh)
             send[h, :, at, c0:c0 + dh] = cut(own_at)
             if nk > 1:
                 zdown[h, :, at, c0:c0 + dh] = cut(0)
@@ -204,11 +206,20 @@
                 zdown[h, :, at, two + c0:two + c0 + dh] = cut(1)
                 zup[h, :, at, c0:c0 + dh] = cut(3)
 
+    together = 2 if tiles % 2 == 0 else 1
+
     def attend_all(h, nk, both):
-        def one(g, carry):
-            attend(h, g, nk, both)
+        def some(g, carry):
+            work = [attend(h, g * together + t, nk, both) for t in range(together)]
+            while work:
+                work = [w for w in work if next(w, True) is None]
             return carry
-        lax.fori_loop(0, tiles, one, 0)
+        lax.fori_loop(0, tiles // together, some, 0)
+
+    def return_rows(h):
+        for k in range(1, spots):
+            back_copy(h, k).start()
+        back[h, r] = send[h, r]
 
     def push(h):
         for k in range(1, spots):
@@ -236,6 +247,7 @@
             attend_all(h, 4, True)
             sums_down(h).start()
             top_back(h).start()
+            return_rows(h)
 
         @pl.when(z == 3)
         def _():
@@ -259,37 +271,45 @@
             top_back(h).wait_recv()
             send[h] = zin[h]
 
-        for k in range(1, spots):
-            back_copy(h, k).start()
-        back[h, r] = send[h, r]
+        @pl.when(z != 2)
+        def _():
+            return_rows(h)
 
     def finish(h):
         cols = columns(h)
-        for k in range(1, spots):
-            back_in(h, k).wait_recv()
-        picked = onehot[h]
-        for c, out in ((0, key_grad), (1, value_grad), (2, query_grad)):
-            block = back[h, :, :, c * dh:(c + 1) * dh].reshape(slots, dh)
-            out[:, cols] = dot(picked, block, 0, 0).astype(BF16)
-        attn = dot(picked, back[h, :, :, 3 * dh:four].reshape(slots, dh), 0, 0).astype(BF16)
-        total[...] += dot(attn, weight[cols, :], 1, 0)
+        for part in range(split):
+            for k in range(1, spots):
+                back_in(h * split + part, k).wait_recv()
+        table = jnp.stack([back[h * split + part] for part in range(split)], axis=1).reshape(slots, four)
+        rows_back = dot(onehot[h], table, 0, 0).astype(BF16)
+        key_grad[:, cols] = rows_back[:, :dh]
+        value_grad[:, cols] = rows_back[:, dh:two]
+        query_grad[:, cols] = rows_back[:, two:two + dh]
+        attn_all[:, cols] = rows_back[:, two + dh:]
+
+        @pl.when(h % pair == pair - 1)
+        def _():
+            both = pl.ds(pl.multiple_of((h - (pair - 1)) * dh, pair * dh), pair * dh)
+            total[...] += dot(attn_all[:, both], weight[both, :], 1, 0)
+
+    pair = 2 if heads % 2 == 0 else 1
 
     def turn(i, carry):
-        @pl.when(i < heads)
+        @pl.when(i < units)
         def _():
             push(i)
 
-        @pl.when(i >= LAG + 1)
-        def _():
-            finish(i - LAG - 1)
-
-        @pl.when(jnp.logical_and(i >= LAG, i < heads + LAG))
+        @pl.when(jnp.logical_and(i >= LAG + 1, (i - LAG - 1) % split == split - 1))
+        def _():
+            finish((i - LAG - 1) // split)
+
+        @pl.when(jnp.logical_and(i >= LAG, i < units + LAG))
         def _():
             give_back(i - LAG)
 
         return carry
 
-    lax.fori_loop(0, heads + LAG + 1, turn, 0)
+    lax.fori_loop(0, units + LAG + 1, turn, 0)
 
     width = layer_out.shape[1]
 
@@ -331,7 +351,7 @@
 
         return carry
 
-    lax.fori_loop(0, heads, settle, 0)
+    lax.fori_loop(0, units, settle, 0)
     for k in range(1, nh):
         share(k).wait()
         mine = mine + half_in[k - 1].astype(F32)
@@ -344,27 +364,31 @@
     dh = wide // heads
     spots = nseq // QUARTERS
     rows = CLUSTERS * MOST // spots
+    split = 2 if rows % 32 == 0 else 1
+    units = heads * split
     model = out_weight.shape[1]
     out = jax.ShapeDtypeStruct((tokens, wide), BF16)
     vm = pl.BlockSpec(memory_space=pltpu.VMEM)
-    full = pltpu.VMEM((heads, spots, rows, 4 * dh), BF16)
+    full = pltpu.VMEM((units, spots, rows // split, 4 * dh), BF16)
     dma = pltpu.SemaphoreType.DMA
     width = model // nh
     return pl.pallas_call(
-        functools.partial(kernel, spots, heads, dh, nh),
+        functools.partial(kernel, spots, heads, split, dh, nh),
         out_shape=(jax.ShapeDtypeStruct((tokens, width), BF16), out, out, out),
-        in_specs=[vm] * 7,
+        in_specs=[vm] * 6,
         out_specs=(vm,) * 4,
         scratch_shapes=[
             pltpu.VMEM((heads, CLUSTERS * MOST, tokens), BF16),
+            pltpu.VMEM((tokens, tokens), BF16),
+            pltpu.VMEM((tokens, wide), BF16),
             full, full, full, full, full, full, full,
             pltpu.VMEM((tokens, model), F32),
             pltpu.VMEM((nh - 1, tokens, width), BF16),
             pltpu.VMEM((nh - 1, tokens, width), BF16),
-            dma((heads, spots)), dma((heads, spots)),
-            dma((heads, 2)), dma((heads, 2)),
-            dma((heads, 2)), dma((heads,)),
-            dma((heads, spots)), dma((heads, spots)),
+            dma((units, spots)), dma((units, spots)),
+            dma((units, 2)), dma((units, 2)),
+            dma((units, 2)), dma((units,)),
+            dma((units, spots)), dma((units, spots)),
             dma((nh - 1,)), dma((nh - 1,)),
         ],
         compiler_params=pltpu.CompilerParams(
@@ -373,7 +397,7 @@
         cost_estimate=pl.CostEstimate(flops=10**10, bytes_accessed=2**24, transcendentals=2**21),
     )(
         query_rows, key_rows, value_rows, out_grad,
-        cluster_ids.reshape(heads, 1, tokens), cluster_ids, out_weight,
+        cluster_ids.reshape(heads, 1, tokens), out_weight,
     )
 
 

time: 170 us -> 179 us (1.053)
  the two profiles are of different devices: /device:TPU:17 before, /device:TPU:0 now
where the time goes in v1:
time: 179 us
  Pallas kernels  171 us (96%)
  local copies, waits for them, and re-layouts  7.14 us (4%)
    pallas_call x1, Pallas kernels, body(): pl.pallas_call(functools.partial(kernel, spots, heads, split, dh, nh), ou...  171 us
    unnamed x6, local copies, waits for them, and re-layouts  7.14 us

profile of v1, /device:TPU:0, one launch (start us, length us, event | category | flops | bytes accessed | tf_op | source)
XLA Modules:
  0.0 179.2 jit_solution(230452178313446202)
XLA Ops:
  0.6 171.4 %shard_map.93 = (bf16[384,1024]{1,0:T(8,128)(2,1)}, bf16[384,1024]{1,0:T(8,128)(2,1)}, bf16[384,1024]{1,0:T(8,128)(2,1)}, bf16[384,1024]{1,0:T(8,128)(2,1)}) custom-call(bf16[384,1024]{1,0:T(8,128)(2,1)} %query.1, bf16[384,1024]{1,0:T(8,128)(2,1)} %key.1, bf16[384,1024]{1,0:T(8,128)(2,1)} %value.1, bf16[384,2048]{1,0:T(8,128)(2,1)} %grad.1, ...), custom_call_target="tpu_custom_call" | custom-call | flops 10000000000 | bytes 16777216 | tf_op jit(solution)/shard_map/pallas_call | solution.py:375
  172.0 0.0 copy-start
  172.1 2.1 %copy.14 = bf16[384,1024]{1,0:T(8,128)(2,1)} copy(bf16[384,1024]{1,0:T(8,128)(2,1)} %get-tuple-element.8) | data formatting | bytes 1572864
  174.2 2.1 %copy.15 = bf16[384,1024]{1,0:T(8,128)(2,1)} copy(bf16[384,1024]{1,0:T(8,128)(2,1)} %get-tuple-element.9) | data formatting | bytes 1572864
  176.3 2.1 %copy.16 = bf16[384,1024]{1,0:T(8,128)(2,1)} copy(bf16[384,1024]{1,0:T(8,128)(2,1)} %get-tuple-element.10) | data formatting | bytes 1572864
  178.3 0.0 copy-done
  178.3 0.9 copy.17
Async XLA Ops:
  172.0 6.3 %copy-start = (bf16[384,1024]{1,0:T(8,128)(2,1)S(1)}, bf16[384,1024]{1,0:T(8,128)(2,1)}, u32[]{:S(2)}) copy-start(bf16[384,1024]{1,0:T(8,128)(2,1)} %get-tuple-element.11) | copy-start | bytes 2359300

commit v2 on v1

--- a/solution.py
+++ b/solution.py
@@ -11,6 +11,7 @@
 MOST = 2
 QUARTERS = 4
 LAG = 6
+AHEAD = 3
 NEGATIVE = -1e30
 MESH = pl.DeviceIdType.MESH
 F32 = jnp.float32
@@ -112,7 +113,7 @@
     at1 = lax.broadcasted_iota(jnp.int32, (tokens, tokens), 1)
     earlier[...] = jnp.where(at0 < at1, 1.0, 0.0).astype(BF16)
 
-    def fill(h, carry):
+    def fill(h):
         cols = columns(h)
         row = ids_row[h]
         named = lax.broadcasted_iota(jnp.int32, (CLUSTERS, tokens), 0) == row
@@ -131,9 +132,7 @@
             for k in range(1, spots):
                 out_copy(u, k).start()
             got[u, r] = send[u, r]
-        return carry
-
-    lax.fori_loop(0, heads, fill, 0)
+
     total[...] = jnp.zeros_like(total)
 
     chunk = min(spots, 4)
@@ -224,19 +223,35 @@
     def push(h):
         for k in range(1, spots):
             in_copy(h, k).wait_recv()
+
+        @pl.when(z == 0)
+        def _():
+            kv_first(h).start()
+
+        @pl.when(z == 1)
+        def _():
+            kv_own(h).start()
+
+        @pl.when(z == 3)
+        def _():
+            top_down(h).start()
+
+    def forward(h):
+        @pl.when(z == 1)
+        def _():
+            kv_forward(h).wait_recv()
+            kv_forward(h).start()
+
+    def compute(h):
         for k in range(1, spots):
             out_copy(h, k).wait_send()
 
         @pl.when(z == 0)
         def _():
-            kv_first(h).start()
             attend_all(h, 1, False)
 
         @pl.when(z == 1)
         def _():
-            kv_own(h).start()
-            kv_forward(h).wait_recv()
-            kv_forward(h).start()
             attend_all(h, 2, False)
 
         @pl.when(z == 2)
@@ -248,10 +263,6 @@
             sums_down(h).start()
             top_back(h).start()
             return_rows(h)
-
-        @pl.when(z == 3)
-        def _():
-            top_down(h).start()
 
     def give_back(h):
         @pl.when(z == 0)
@@ -294,22 +305,29 @@
 
     pair = 2 if heads % 2 == 0 else 1
 
-    def turn(i, carry):
-        @pl.when(i < units)
-        def _():
-            push(i)
-
-        @pl.when(jnp.logical_and(i >= LAG + 1, (i - LAG - 1) % split == split - 1))
-        def _():
-            finish((i - LAG - 1) // split)
-
-        @pl.when(jnp.logical_and(i >= LAG, i < units + LAG))
-        def _():
-            give_back(i - LAG)
-
+    def turn(t, carry):
+        def stage(lag, run):
+            @pl.when(jnp.logical_and(t >= lag, t < units + lag))
+            def _():
+                run(t - lag)
+
+        @pl.when(jnp.logical_and(t < units, t % split == 0))
+        def _():
+            fill(t // split)
+
+        stage(AHEAD, push)
+        stage(AHEAD + 1, forward)
+        stage(AHEAD + 2, compute)
+        last = AHEAD + 2 + LAG + 1
+
+        @pl.when(jnp.logical_and(t >= last, (t - last) % split == split - 1))
+        def _():
+            finish((t - last) // split)
+
+        stage(AHEAD + 2 + LAG, give_back)
         return carry
 
-    lax.fori_loop(0, units + LAG + 1, turn, 0)
+    lax.fori_loop(0, units + AHEAD + LAG + 3, turn, 0)
 
     width = layer_out.shape[1]
 
@@ -356,6 +374,24 @@
         share(k).wait()
         mine = mine + half_in[k - 1].astype(F32)
     layer_out[...] = mine.astype(BF16)
+
+
+def hand_out(*refs):
+    count = len(refs) // 2
+    sems = refs[-1]
+    parts = 4
+    size = refs[0].shape[0] // parts
+    copies = [
+        pltpu.make_async_copy(
+            refs[a].at[pl.ds(b * size, size)], refs[count + a].at[pl.ds(b * size, size)], sems.at[a, b]
+        )
+        for a in range(count)
+        for b in range(parts)
+    ]
+    for copy in copies:
+        copy.start()
+    for copy in copies:
+        copy.wait()
 
 
 def body(nseq, nh, query_rows, key_rows, value_rows, out_grad, cluster_ids, out_weight):
@@ -372,7 +408,7 @@
     full = pltpu.VMEM((units, spots, rows // split, 4 * dh), BF16)
     dma = pltpu.SemaphoreType.DMA
     width = model // nh
-    return pl.pallas_call(
+    results = pl.pallas_call(
         functools.partial(kernel, spots, heads, split, dh, nh),
         out_shape=(jax.ShapeDtypeStruct((tokens, width), BF16), out, out, out),
         in_specs=[vm] * 6,
@@ -399,6 +435,14 @@
         query_rows, key_rows, value_rows, out_grad,
         cluster_ids.reshape(heads, 1, tokens), out_weight,
     )
+    anywhere = pl.BlockSpec(memory_space=pl.ANY)
+    return pl.pallas_call(
+        hand_out,
+        out_shape=tuple(jax.ShapeDtypeStruct(x.shape, x.dtype) for x in results),
+        in_specs=[anywhere] * 4,
+        out_specs=(anywhere,) * 4,
+        scratch_shapes=[dma((4, 4))],
+    )(*results)
 
 
 def solution(mesh):

time: 179 us -> 231 us (1.29)
  Pallas kernels: 171 us -> 230 us
  local copies, waits for them, and re-layouts: 7.14 us -> 0 us
    pallas_call x0 -> x1, Pallas kernels: none -> 96.5 us  [body(): pl.pallas_call(hand_out, out_shape=tuple((jax.ShapeDtypeStruct(x.shape, x...]
    pallas_call x1, Pallas kernels: 171 us -> 134 us  [body(): pl.pallas_call(functools.partial(kernel, spots, heads, split, dh, nh), ou...]
    unnamed x6 -> x0, local copies, waits for them, and re-layouts: 7.14 us -> none
where the time goes in v2:
time: 231 us
  Pallas kernels  230 us (100%)
    pallas_call x1, Pallas kernels, body(): pl.pallas_call(functools.partial(kernel, spots, heads, split, dh, nh), ou...  134 us
    pallas_call x1, Pallas kernels, body(): pl.pallas_call(hand_out, out_shape=tuple((jax.ShapeDtypeStruct(x.shape, x...  96.5 us

profile of v2, /device:TPU:0, one launch (start us, length us, event | category | flops | bytes accessed | tf_op | source)
XLA Modules:
  0.0 231.1 jit_solution(7896825088512754671)
XLA Ops:
  0.6 134.0 %shard_map.93 = (bf16[384,1024]{1,0:T(8,128)(2,1)}, bf16[384,1024]{1,0:T(8,128)(2,1)}, bf16[384,1024]{1,0:T(8,128)(2,1)}, bf16[384,1024]{1,0:T(8,128)(2,1)}) custom-call(bf16[384,1024]{1,0:T(8,128)(2,1)} %query.1, bf16[384,1024]{1,0:T(8,128)(2,1)} %key.1, bf16[384,1024]{1,0:T(8,128)(2,1)} %value.1, bf16[384,2048]{1,0:T(8,128)(2,1)} %grad.1, ...), custom_call_target="tpu_custom_call" | custom-call | flops 10000000000 | bytes 16777216 | tf_op jit(solution)/shard_map/pallas_call | solution.py:411
  134.6 96.5 %shard_map.94 = (bf16[384,1024]{1,0:T(8,128)(2,1)}, bf16[384,1024]{1,0:T(8,128)(2,1)}, bf16[384,1024]{1,0:T(8,128)(2,1)}, bf16[384,1024]{1,0:T(8,128)(2,1)}) custom-call(bf16[384,1024]{1,0:T(8,128)(2,1)} %get-tuple-element.8.refs_0_, bf16[384,1024]{1,0:T(8,128)(2,1)} %get-tuple-element.9.refs_1_, bf16[384,1024]{1,0:T(8,128)(2,1)} %get-tuple-element.10.refs_2_, ...), custom_call_target="tpu_custom_call" | custom-call | tf_op jit(solution)/shard_map/pallas_call | solution.py:439

commit v3 on v2

--- a/solution.py
+++ b/solution.py
@@ -26,7 +26,7 @@
     spots, heads, split, dh, nh,
     query, key, value, grad, ids_row, weight,
     layer_out, query_grad, key_grad, value_grad,
-    onehot, earlier, attn_all, send, got, kv, zin, zup, zdown, back, total, half_out, half_in,
+    onehot, earlier, attn_all, allow, send, got, kv, zin, zup, zdown, back, total, half_out, half_in,
     as_, ar, kvs, kvr, zs, zr, bs, br, hs, hr,
 ):
     tokens = query.shape[0]
@@ -141,6 +141,20 @@
     def flat(x):
         return x.reshape(x.shape[0] * step, x.shape[2])
 
+    def causal(nkeys, nq, own_at, c):
+        half = chunk * step
+        j = lax.broadcasted_iota(jnp.int32, (nkeys, nq), 0)
+        i = lax.broadcasted_iota(jnp.int32, (nkeys, nq), 1)
+        second = (i >= half).astype(jnp.int32)
+        src = c * chunk + ((i - second * half) >> 4)
+        rank_q = ((own_at + second) * spots + src) * 2 + (i & 1)
+        rank_k = (j >> 4) * 2 + (j & 1)
+        same = ((j & 15) >> 1) == ((i & 15) >> 1)
+        return jnp.where(jnp.logical_and(same, rank_k <= rank_q), 1.0, 0.0)
+
+    if chunks == 1:
+        allow[:, :2 * chunk * step] = causal(4 * quarter, 2 * chunk * step, 2, 0)
+
     def attend(h, g, nk, both):
         at = pl.ds(pl.multiple_of(g * step, step), step)
         own = flat(got[h, :, at, low])
@@ -155,12 +169,8 @@
         nkeys = nk * quarter
         half = chunk * step
         nq = half * (2 if both else 1)
-        j = lax.broadcasted_iota(jnp.int32, (nkeys, 1), 0)
-        occupied = jnp.max(jnp.abs(keys.astype(F32)), axis=1, keepdims=True) > 0
-        cluster_k = jnp.where(occupied, (j & 15) >> 1, -1)
-        rank_k = (j >> 4) * 2 + (j & 1)
-        i = lax.broadcasted_iota(jnp.int32, (1, nq), 1)
-        cluster_q = (i & 15) >> 1
+        lit = jnp.where(keys != 0, 1, 0).astype(BF16)
+        occupied = dot(lit, jnp.ones((dh, nq), BF16), 1, 0)
         own_at = nk - (2 if both else 1)
         dk = dv = None
         for c in range(chunks):
@@ -173,11 +183,12 @@
             raw = dot(keys, q, 1, 1)
             dprob = dot(values, dout, 1, 1)
             yield
-            second = (i >= half).astype(jnp.int32) if both else 0
-            src = c * chunk + ((i - second * half) >> 4)
-            rank_q = ((own_at + second) * spots + src) * 2 + (i & 1)
-            allowed = jnp.logical_and(cluster_k == cluster_q, rank_k <= rank_q)
-            scores = jnp.where(allowed, raw * scale, NEGATIVE)
+            if chunks == 1:
+                top = 0 if both else 3 - nk
+                seen = allow[top * quarter:(top + nk) * quarter, :nq]
+            else:
+                seen = causal(nkeys, nq, own_at, c)
+            scores = jnp.where(occupied * seen > 0, raw * scale, NEGATIVE)
             w = jnp.exp(scores - jnp.max(scores, axis=0, keepdims=True))
             probs = w * (1.0 / jnp.sum(w, axis=0, keepdims=True))
             probs_half = probs.astype(BF16)
@@ -378,20 +389,8 @@
 
 def hand_out(*refs):
     count = len(refs) // 2
-    sems = refs[-1]
-    parts = 4
-    size = refs[0].shape[0] // parts
-    copies = [
-        pltpu.make_async_copy(
-            refs[a].at[pl.ds(b * size, size)], refs[count + a].at[pl.ds(b * size, size)], sems.at[a, b]
-        )
-        for a in range(count)
-        for b in range(parts)
-    ]
-    for copy in copies:
-        copy.start()
-    for copy in copies:
-        copy.wait()
+    for a in range(count):
+        refs[count + a][...] = refs[a][...]
 
 
 def body(nseq, nh, query_rows, key_rows, value_rows, out_grad, cluster_ids, out_weight):
@@ -417,6 +416,7 @@
             pltpu.VMEM((heads, CLUSTERS * MOST, tokens), BF16),
             pltpu.VMEM((tokens, tokens), BF16),
             pltpu.VMEM((tokens, wide), BF16),
+            pltpu.VMEM((4 * 16 * spots, 128), F32) if spots <= 4 else pltpu.VMEM((8, 128), F32),
             full, full, full, full, full, full, full,
             pltpu.VMEM((tokens, model), F32),
             pltpu.VMEM((nh - 1, tokens, width), BF16),
@@ -435,13 +435,14 @@
         query_rows, key_rows, value_rows, out_grad,
         cluster_ids.reshape(heads, 1, tokens), out_weight,
     )
-    anywhere = pl.BlockSpec(memory_space=pl.ANY)
+    blocks = [pl.BlockSpec((tokens // 4, x.shape[1]), lambda i: (i, 0)) for x in results]
     return pl.pallas_call(
         hand_out,
+        grid=(4,),
         out_shape=tuple(jax.ShapeDtypeStruct(x.shape, x.dtype) for x in results),
-        in_specs=[anywhere] * 4,
-        out_specs=(anywhere,) * 4,
-        scratch_shapes=[dma((4, 4))],
+        in_specs=blocks,
+        out_specs=tuple(blocks),
+        compiler_params=pltpu.CompilerParams(vmem_limit_bytes=16 * 2**20),
     )(*results)
 
 

time: 231 us -> 142 us (0.61)
  Pallas kernels: 230 us -> 136 us
  local copies, waits for them, and re-layouts: 0 us -> 4.52 us
    pallas_call x1, Pallas kernels: 96.5 us -> 2.1 us  [body(): pl.pallas_call(hand_out, grid=(4,), out_shape=tuple((jax.ShapeDtypeStruct...]
    unnamed x0 -> x8, local copies, waits for them, and re-layouts: none -> 4.52 us
where the time goes in v3:
time: 142 us; the launch traced here: 141 us
  Pallas kernels  136 us (96%)
  local copies, waits for them, and re-layouts  4.52 us (3%)
    pallas_call x1, Pallas kernels, body(): pl.pallas_call(functools.partial(kernel, spots, heads, split, dh, nh), ou...  134 us
    unnamed x8, local copies, waits for them, and re-layouts  4.52 us

profile of v3, /device:TPU:0, one launch (start us, length us, event | category | flops | bytes accessed | tf_op | source)
XLA Modules:
  0.0 141.3 jit_solution(2989228981340120500)
XLA Ops:
  0.6 134.0 %shard_map.93 = (bf16[384,1024]{1,0:T(8,128)(2,1)}, bf16[384,1024]{1,0:T(8,128)(2,1)}, bf16[384,1024]{1,0:T(8,128)(2,1)}, bf16[384,1024]{1,0:T(8,128)(2,1)}) custom-call(bf16[384,1024]{1,0:T(8,128)(2,1)} %query.1, bf16[384,1024]{1,0:T(8,128)(2,1)} %key.1, bf16[384,1024]{1,0:T(8,128)(2,1)} %value.1, bf16[384,2048]{1,0:T(8,128)(2,1)} %grad.1, ...), custom_call_target="tpu_custom_call" | custom-call | flops 10000000000 | bytes 16777216 | tf_op jit(solution)/shard_map/pallas_call | solution.py:410
  134.6 0.0 copy-start
  134.6 1.1 copy-done
  135.8 0.0 copy-start.1
  135.8 1.1 copy-done.1
  136.9 0.0 copy-start.2
  136.9 1.1 copy-done.2
  138.0 0.0 copy-start.3
  138.0 1.1 copy-done.3
  139.2 2.1 %shard_map.94 = (bf16[384,1024]{1,0:T(8,128)(2,1)}, bf16[384,1024]{1,0:T(8,128)(2,1)}, bf16[384,1024]{1,0:T(8,128)(2,1)}, bf16[384,1024]{1,0:T(8,128)(2,1)}) custom-call(bf16[384,1024]{1,0:T(8,128)(2,1)S(1)} %copy-done, bf16[384,1024]{1,0:T(8,128)(2,1)S(1)} %copy-done.1, bf16[384,1024]{1,0:T(8,128)(2,1)S(1)} %copy-done.2, bf16[384,1024]{1,0:T(8,128)(2,1)S(1)} %copy-done.3), custom_call_target="tpu_custom_call" | custom-call | tf_op jit(solution)/shard_map/pallas_call | solution.py:439
Async XLA Ops:
  134.6 1.1 copy-start
  135.8 1.1 copy-start.1
  136.9 1.1 copy-start.2
  138.0 1.1 copy-start.3

commit v4 on v3

--- a/solution.py
+++ b/solution.py
@@ -11,6 +11,7 @@
 MOST = 2
 QUARTERS = 4
 LAG = 6
+LAG_LOWEST = 8
 AHEAD = 3
 NEGATIVE = -1e30
 MESH = pl.DeviceIdType.MESH
@@ -329,16 +330,17 @@
         stage(AHEAD, push)
         stage(AHEAD + 1, forward)
         stage(AHEAD + 2, compute)
-        last = AHEAD + 2 + LAG + 1
-
-        @pl.when(jnp.logical_and(t >= last, (t - last) % split == split - 1))
-        def _():
-            finish((t - last) // split)
-
-        stage(AHEAD + 2 + LAG, give_back)
+        back_at = AHEAD + 2 + jnp.where(z == 0, LAG_LOWEST, LAG)
+        done = t - back_at - 1
+
+        @pl.when(jnp.logical_and(jnp.logical_and(done >= 0, done < units), done % split == split - 1))
+        def _():
+            finish(done // split)
+
+        stage(back_at, give_back)
         return carry
 
-    lax.fori_loop(0, units + AHEAD + LAG + 3, turn, 0)
+    lax.fori_loop(0, units + AHEAD + LAG_LOWEST + 3, turn, 0)
 
     width = layer_out.shape[1]
 
@@ -442,7 +444,7 @@
         out_shape=tuple(jax.ShapeDtypeStruct(x.shape, x.dtype) for x in results),
         in_specs=blocks,
         out_specs=tuple(blocks),
-        compiler_params=pltpu.CompilerParams(vmem_limit_bytes=16 * 2**20),
+        compiler_params=pltpu.CompilerParams(vmem_limit_bytes=60 * 2**20),
     )(*results)
 
 

time: 142 us -> 139 us (0.979)
  local copies, waits for them, and re-layouts: 4.52 us -> 0 us
  Pallas kernels: 136 us -> 138 us
    unnamed x8 -> x0, local copies, waits for them, and re-layouts: 4.52 us -> none
    pallas_call x1, Pallas kernels: 2.1 us -> 4.24 us  [body(): pl.pallas_call(hand_out, grid=(4,), out_shape=tuple((jax.ShapeDtypeStruct...]
where the time goes in v4:
time: 139 us
  Pallas kernels  138 us (99%)
    pallas_call x1, Pallas kernels, body(): pl.pallas_call(functools.partial(kernel, spots, heads, split, dh, nh), ou...  134 us
    pallas_call x1, Pallas kernels, body(): pl.pallas_call(hand_out, grid=(4,), out_shape=tuple((jax.ShapeDtypeStruct...  4.24 us

profile of v4, /device:TPU:0, one launch (start us, length us, event | category | flops | bytes accessed | tf_op | source)
XLA Modules:
  0.0 138.8 jit_solution(13796453892224379286)
XLA Ops:
  0.6 133.9 %shard_map.93 = (bf16[384,1024]{1,0:T(8,128)(2,1)}, bf16[384,1024]{1,0:T(8,128)(2,1)}, bf16[384,1024]{1,0:T(8,128)(2,1)}, bf16[384,1024]{1,0:T(8,128)(2,1)}) custom-call(bf16[384,1024]{1,0:T(8,128)(2,1)} %query.1, bf16[384,1024]{1,0:T(8,128)(2,1)} %key.1, bf16[384,1024]{1,0:T(8,128)(2,1)} %value.1, bf16[384,2048]{1,0:T(8,128)(2,1)} %grad.1, ...), custom_call_target="tpu_custom_call" | custom-call | flops 10000000000 | bytes 16777216 | tf_op jit(solution)/shard_map/pallas_call | solution.py:412
  134.6 4.2 %shard_map.94 = (bf16[384,1024]{1,0:T(8,128)(2,1)}, bf16[384,1024]{1,0:T(8,128)(2,1)}, bf16[384,1024]{1,0:T(8,128)(2,1)}, bf16[384,1024]{1,0:T(8,128)(2,1)}) custom-call(bf16[384,1024]{1,0:T(8,128)(2,1)} %get-tuple-element.8.refs_0_, bf16[384,1024]{1,0:T(8,128)(2,1)} %get-tuple-element.9.refs_1_, bf16[384,1024]{1,0:T(8,128)(2,1)} %get-tuple-element.10.refs_2_, ...), custom_call_target="tpu_custom_call" | custom-call | tf_op jit(solution)/shard_map/pallas_call | solution.py:441

commit v5 on v4

--- a/solution.py
+++ b/solution.py
@@ -10,8 +10,8 @@
 CLUSTERS = 256
 MOST = 2
 QUARTERS = 4
-LAG = 6
-LAG_LOWEST = 8
+LAG = 8
+LAG_LOWEST = 11
 AHEAD = 3
 NEGATIVE = -1e30
 MESH = pl.DeviceIdType.MESH
@@ -401,7 +401,7 @@
     dh = wide // heads
     spots = nseq // QUARTERS
     rows = CLUSTERS * MOST // spots
-    split = 2 if rows % 32 == 0 else 1
+    split = max(s for s in (1, 2, 4) if rows % (16 * s) == 0)
     units = heads * split
     model = out_weight.shape[1]
     out = jax.ShapeDtypeStruct((tokens, wide), BF16)

time: 139 us -> 135 us (0.971)
  Pallas kernels: 138 us -> 134 us
    pallas_call x1, Pallas kernels: 134 us -> 130 us  [body(): pl.pallas_call(functools.partial(kernel, spots, heads, split, dh, nh), ou...]
where the time goes in v5:
time: 135 us
  Pallas kernels  134 us (99%)
    pallas_call x1, Pallas kernels, body(): pl.pallas_call(functools.partial(kernel, spots, heads, split, dh, nh), ou...  130 us
    pallas_call x1, Pallas kernels, body(): pl.pallas_call(hand_out, grid=(4,), out_shape=tuple((jax.ShapeDtypeStruct...  4.24 us

profile of v5, /device:TPU:0, one launch (start us, length us, event | category | flops | bytes accessed | tf_op | source)
XLA Modules:
  0.0 134.8 jit_solution(666318139084138542)
XLA Ops:
  0.6 129.9 %shard_map.93 = (bf16[384,1024]{1,0:T(8,128)(2,1)}, bf16[384,1024]{1,0:T(8,128)(2,1)}, bf16[384,1024]{1,0:T(8,128)(2,1)}, bf16[384,1024]{1,0:T(8,128)(2,1)}) custom-call(bf16[384,1024]{1,0:T(8,128)(2,1)} %query.1, bf16[384,1024]{1,0:T(8,128)(2,1)} %key.1, bf16[384,1024]{1,0:T(8,128)(2,1)} %value.1, bf16[384,2048]{1,0:T(8,128)(2,1)} %grad.1, ...), custom_call_target="tpu_custom_call" | custom-call | flops 10000000000 | bytes 16777216 | tf_op jit(solution)/shard_map/pallas_call | solution.py:412
  130.5 4.2 %shard_map.94 = (bf16[384,1024]{1,0:T(8,128)(2,1)}, bf16[384,1024]{1,0:T(8,128)(2,1)}, bf16[384,1024]{1,0:T(8,128)(2,1)}, bf16[384,1024]{1,0:T(8,128)(2,1)}) custom-call(bf16[384,1024]{1,0:T(8,128)(2,1)} %get-tuple-element.8.refs_0_, bf16[384,1024]{1,0:T(8,128)(2,1)} %get-tuple-element.9.refs_1_, bf16[384,1024]{1,0:T(8,128)(2,1)} %get-tuple-element.10.refs_2_, ...), custom_call_target="tpu_custom_call" | custom-call | tf_op jit(solution)/shard_map/pallas_call | solution.py:441

commit v6 on v5

--- a/solution.py
+++ b/solution.py
@@ -327,8 +327,8 @@
         def _():
             fill(t // split)
 
+        stage(AHEAD + 1, forward)
         stage(AHEAD, push)
-        stage(AHEAD + 1, forward)
         stage(AHEAD + 2, compute)
         back_at = AHEAD + 2 + jnp.where(z == 0, LAG_LOWEST, LAG)
         done = t - back_at - 1
@@ -437,10 +437,10 @@
         query_rows, key_rows, value_rows, out_grad,
         cluster_ids.reshape(heads, 1, tokens), out_weight,
     )
-    blocks = [pl.BlockSpec((tokens // 4, x.shape[1]), lambda i: (i, 0)) for x in results]
+    blocks = [pl.BlockSpec((tokens // 8, x.shape[1]), lambda i: (i, 0)) for x in results]
     return pl.pallas_call(
         hand_out,
-        grid=(4,),
+        grid=(8,),
         out_shape=tuple(jax.ShapeDtypeStruct(x.shape, x.dtype) for x in results),
         in_specs=blocks,
         out_specs=tuple(blocks),

time: 135 us -> 137 us (1.015)
  Pallas kernels: 134 us -> 136 us
    pallas_call x1, Pallas kernels: 4.24 us -> 6.26 us  [body(): pl.pallas_call(hand_out, grid=(8,), out_shape=tuple((jax.ShapeDtypeStruct...]
where the time goes in v6:
time: 137 us
  Pallas kernels  136 us (99%)
    pallas_call x1, Pallas kernels, body(): pl.pallas_call(functools.partial(kernel, spots, heads, split, dh, nh), ou...  130 us
    pallas_call x1, Pallas kernels, body(): pl.pallas_call(hand_out, grid=(8,), out_shape=tuple((jax.ShapeDtypeStruct...  6.26 us

profile of v6, /device:TPU:0, one launch (start us, length us, event | category | flops | bytes accessed | tf_op | source)
XLA Modules:
  0.0 136.6 jit_solution(13891462861831070324)
XLA Ops:
  0.6 129.7 %shard_map.93 = (bf16[384,1024]{1,0:T(8,128)(2,1)}, bf16[384,1024]{1,0:T(8,128)(2,1)}, bf16[384,1024]{1,0:T(8,128)(2,1)}, bf16[384,1024]{1,0:T(8,128)(2,1)}) custom-call(bf16[384,1024]{1,0:T(8,128)(2,1)} %query.1, bf16[384,1024]{1,0:T(8,128)(2,1)} %key.1, bf16[384,1024]{1,0:T(8,128)(2,1)} %value.1, bf16[384,2048]{1,0:T(8,128)(2,1)} %grad.1, ...), custom_call_target="tpu_custom_call" | custom-call | flops 10000000000 | bytes 16777216 | tf_op jit(solution)/shard_map/pallas_call | solution.py:412
  130.3 6.3 %shard_map.94 = (bf16[384,1024]{1,0:T(8,128)(2,1)}, bf16[384,1024]{1,0:T(8,128)(2,1)}, bf16[384,1024]{1,0:T(8,128)(2,1)}, bf16[384,1024]{1,0:T(8,128)(2,1)}) custom-call(bf16[384,1024]{1,0:T(8,128)(2,1)} %get-tuple-element.8.refs_0_, bf16[384,1024]{1,0:T(8,128)(2,1)} %get-tuple-element.9.refs_1_, bf16[384,1024]{1,0:T(8,128)(2,1)} %get-tuple-element.10.refs_2_, ...), custom_call_target="tpu_custom_call" | custom-call | tf_op jit(solution)/shard_map/pallas_call | solution.py:441
